TPU v7x, 32 devices: a whole 2x2x4 slice. The times are simulated.
32 devices in a mesh: groups: 2 (over y), cells: 4 (over z), tm: 2 (over x), cls: 2 (over core).
Axes of the slice: x: 2, y: 2, z: 4, core: 2. Of those that a mesh axis runs over, the one named last changes fastest.
Arguments:
- start_density: float32 [128, 4096], P(('groups', 'cls'), 'cells'), parts along dimension 0, may hold values from 0.1 to 2
- final_value: float32 [128, 4096], P(('groups', 'cls'), 'cells'), parts along dimension 0, may hold values from 0 to 212
- congestion: float32 [4, 4096], P(('groups', 'tm'), 'cells'), parts along dimension 0, may hold values from 0.1 to 10
- capacity: float32 [8192], P(('groups', 'cells')), parts along dimension 0, may hold values from 0.5 to 4
- trans_values: bfloat16 [64, 128, 128], P(('groups', 'cells')), parts along dimension 0, may hold values from 0.00015544891 to 0.0046691895
- src_local: int32 [64], P(('groups', 'cells')), parts along dimension 0, may hold values from 0 to 7
- dst_local: int32 [64], P(('groups', 'cells')), parts along dimension 0, may hold values from 0 to 7
- bucket_len: int32 [32], P(('groups', 'cells')), parts along dimension 0, may hold values from 0 to 2, as said below
Outputs:
- density: float32 [4, 64, 4096], P(('groups', 'tm'), 'cls', 'cells'), parts along dimension 0
- class_mean: float32 [4, 4096], P(('groups', 'tm'), 'cells'), parts along dimension 0
- values: float32 [4, 64, 4096], P(('groups', 'tm'), 'cls', 'cells'), parts along dimension 0
There are 2 independent parts, one for each index of `groups`. A program takes and returns all parts, laid end to end along the dimension named above; each array names one. Nothing has to cross between parts.
Inputs may be any that keep to these rules, and one draw needn't show every extreme that they name: bucket_len[d * 4 + d] = 2 for every owner d: each owner has 2 live slots into its own blocks.
All inputs are finite; a program needn't handle non-finite values.
Results may differ from a plain program's by a relative error of at most 0.00071.
Values may be sent and summed in bfloat16 or wider, within the bound.
A program may use at most 64 MiB of HBM per device.

v0:
```python
import jax
import jax.numpy as jnp
from jax import lax
from jax.sharding import PartitionSpec as P

BS = 128
CLASSES = 64


softness = 1.0
base_cost = 0.05
far_below = -1e30


def from_behind(shard, axis, by):
    size = lax.axis_size(axis)
    pairs = [(i, i + by) for i in range(size) if 0 <= i + by < size]
    return lax.ppermute(shard, axis, pairs)


def shards(
    start_density, final_value, congestion, capacity, trans_values, src_local, dst_local, bucket_len
):
    sections = lax.axis_size("tm")
    section_index = lax.axis_index("tm")
    owners = lax.axis_size("cells")
    class_count, cell_count = start_density.shape
    block_count = cell_count // BS
    edge_count = src_local.shape[0]
    per_peer = edge_count // owners
    position = jnp.arange(edge_count, dtype=jnp.int32)
    active_slot = position % per_peer < jnp.repeat(bucket_len, per_peer)
    target_block = jnp.where(active_slot, dst_local, -1)
    arrived = lax.all_to_all(target_block, "cells", split_axis=0, concat_axis=0, tiled=True)
    block_ids = jnp.arange(block_count, dtype=jnp.int32)
    gather_hot = (arrived[:, None] == block_ids[None, :]).astype(jnp.bfloat16)
    into_hot = jnp.transpose(gather_hot)
    src_hot = src_local[None, :] == block_ids[:, None]
    src_float = src_hot.astype(jnp.float32)

    def advance(masses, mobility_now):
        moving = (masses * mobility_now).astype(jnp.bfloat16)
        picked = jnp.take(moving, src_local, axis=1)
        partial_value = jnp.einsum(
            "ceb,ebk->eck", picked, trans_values, preferred_element_type=jnp.float32
        ).astype(jnp.bfloat16)
        received = lax.all_to_all(partial_value, "cells", split_axis=0, concat_axis=0, tiled=True)
        inflow = jnp.einsum("ae,ecb->cab", into_hot, received, preferred_element_type=jnp.float32)
        return masses * (1.0 - mobility_now) + inflow

    def retreat(values_now, travel_now):
        block_low = jnp.min(values_now, axis=2).astype(jnp.bfloat16)
        low_wide = lax.optimization_barrier(block_low).astype(jnp.float32)
        weight = jnp.exp(-(values_now - low_wide[:, :, None]) / softness).astype(jnp.bfloat16)
        sent_weight = jnp.einsum(
            "ea,cab->ecb", gather_hot, weight, preferred_element_type=jnp.float32
        ).astype(jnp.bfloat16)
        sent_low = jnp.einsum(
            "ea,ca->ec", gather_hot, block_low, preferred_element_type=jnp.float32
        ).astype(jnp.bfloat16)
        weight_back, low_back = (
            lax.all_to_all(sent_weight, "cells", split_axis=0, concat_axis=0, tiled=True),
            lax.all_to_all(sent_low, "cells", split_axis=0, concat_axis=0, tiled=True),
        )
        kernel_sums = jnp.einsum(
            "eij,ecj->cei", trans_values, weight_back, preferred_element_type=jnp.float32
        )
        edge_log = jnp.where(
            active_slot[None, :], -jnp.transpose(low_back).astype(jnp.float32) / softness, far_below
        )
        block_top = jnp.max(jnp.where(src_hot[None, :, :], edge_log[:, None, :], far_below), axis=2)
        stay_log = -values_now / softness
        ceiling = jnp.maximum(stay_log, block_top[:, :, None])
        ceiling_src = jnp.take(ceiling, src_local, axis=1)
        edge_terms = jnp.exp(edge_log[:, :, None] - ceiling_src) * kernel_sums
        edge_total = jnp.einsum(
            "ae,ceb->cab", src_float, edge_terms, precision=lax.Precision.HIGHEST
        )
        grand_total = jnp.exp(stay_log - ceiling) + edge_total
        return travel_now - softness * (ceiling + jnp.log(grand_total))

    start_blocks = start_density.reshape(class_count, block_count, BS)
    final_blocks = final_value.reshape(class_count, block_count, BS)
    loading = congestion.reshape(congestion.shape[0], block_count, BS) / capacity.reshape(
        1, block_count, BS
    )
    mobility = 1.0 / (1.0 + loading)
    travel = base_cost * (1.0 + loading)
    step_count = congestion.shape[0]
    pieces = 1
    portion_size = class_count // pieces
    rounds = sections + pieces - 1

    def forward_round(round_index, carried):
        incoming, archive = carried
        batch_index = round_index - section_index
        active = (batch_index >= 0) & (batch_index < pieces)
        offset = jnp.clip(batch_index, 0, pieces - 1) * portion_size
        masses = jnp.where(section_index == 0, start_blocks, incoming)
        masses = advance(masses, mobility[0])
        outputs = [masses]
        stacked = jnp.stack(outputs)
        previous = archive
        archive = lax.dynamic_update_slice_in_dim(
            archive, jnp.where(active, stacked, previous), offset, 1
        )
        incoming = from_behind(masses, "tm", 1)
        return (incoming, archive)

    def backward_round(round_index, carried):
        incoming, archive = carried
        batch_index = round_index - (sections - 1 - section_index)
        active = (batch_index >= 0) & (batch_index < pieces)
        offset = jnp.clip(batch_index, 0, pieces - 1) * portion_size
        values_now = jnp.where(section_index == sections - 1, final_blocks, incoming)
        outputs = [None] * step_count
        for moment in reversed(range(step_count)):
            values_now = retreat(values_now, travel[moment])
            outputs[moment] = values_now
        stacked = jnp.stack(outputs)
        previous = archive
        archive = lax.dynamic_update_slice_in_dim(
            archive, jnp.where(active, stacked, previous), offset, 1
        )
        incoming = from_behind(values_now, "tm", -1)
        return (incoming, archive)

    empty_state = jnp.zeros((portion_size, block_count, BS), jnp.float32)
    empty_archive = jnp.zeros((step_count, class_count, block_count, BS), jnp.float32)

    def both_rounds(round_index, carried):
        return (forward_round(round_index, carried[0]), backward_round(round_index, carried[1]))

    forward_done, backward_done = lax.fori_loop(
        0, rounds, both_rounds, ((empty_state, empty_archive), (empty_state, empty_archive))
    )
    density_blocks = forward_done[1]
    value_blocks = backward_done[1]
    local_steps = density_blocks.shape[0]
    density = density_blocks.reshape(local_steps, class_count, cell_count)
    class_mean = lax.psum(jnp.sum(density, axis=1), "cls") / CLASSES
    values = value_blocks.reshape(local_steps, class_count, cell_count)
    return (density, class_mean, values)


def solution(mesh):
    in_specs = (
        P(("groups", "cls"), "cells"),
        P(("groups", "cls"), "cells"),
        P(("groups", "tm"), "cells"),
        P(("groups", "cells")),
        P(("groups", "cells"), None, None),
        P(("groups", "cells")),
        P(("groups", "cells")),
        P(("groups", "cells")),
    )
    out_specs = (
        P(("groups", "tm"), "cls", "cells"),
        P(("groups", "tm"), "cells"),
        P(("groups", "tm"), "cls", "cells"),
    )
    return jax.shard_map(shards, mesh=mesh, in_specs=in_specs, out_specs=out_specs, check_vma=False)
```

profile of v0, /device:TPU:0, one launch (start us, length us, event | category | flops | bytes accessed | tf_op | source)
XLA Modules:
  0.0 88.9 jit_solution(9508613148728367477)
XLA Ops:
  0.7 1.0 %copy.30 = f32[4,8,8,128]{3,2,1,0:T(8,128)S(1)} copy(f32[4,8,8,128]{3,1,2,0:T(8,128)} %bitcast.137) | data formatting | bytes 262144
  2.5 11.7 %all_to_all.57 = s32[4,2,1]{1,2,0:T(1,128)S(1)} all-to-all(s32[4,2,1]{1,2,0:T(1,128)S(1)} %bitcast.140), channel_id=1, replica_groups=mesh['groups'=2,'cells'=4,'tm'=2,'cls'=2] {'cells'}, dimensions={0} | all-to-all | bytes 64 | tf_op jit(solution)/shard_map/all_to_all | solution.py:34
  16.1 68.3 %while.23 = (s32[]{:T(128)}, f32[32,8,128]{2,1,0:T(8,128)S(1)}, f32[1,32,8,128]{3,2,1,0:T(8,128)S(1)}, f32[32,8,128]{2,1,0:T(8,128)S(1)}, f32[1,32,8,128]{3,2,1,...) while((s32[]{:T(128)}, f32[32,8,128]{2,1,0:T(8,128)S(1)}, ...), condition=%wide.region_3.4_spmd.clone.clone.clone, body=%wide.region_0.3_spmd.clone.clone.clone.sunk | while | flops 21933516 | bytes 5943367 | solution.py:134
  17.0 3.2 %all-to-all-start.2 = ((bf16[4,2,32]{2,1,0:T(2,128)(2,1)}), bf16[4,2,32]{2,1,0:T(2,128)(2,1)S(1)}, u32[]{:S(2)}, u32[]{:S(2)}) async-start(bf16[4,2,32]{2,1,0:T(2,128)(2,1)} %bitcast.126), calls=%async_computation.2 | async-start | bytes 4096 | tf_op jit(solution)/shard_map/while/body/eval_jaxpr/all_to_all | solution.py:63
  21.3 0.9 convolution_convert_fusion.5
  22.8 2.8 %all-to-all-done.2 = bf16[4,2,32]{2,1,0:T(2,128)(2,1)S(1)} async-done(((bf16[4,2,32]{2,1,0:T(2,128)(2,1)}), bf16[4,2,32]{2,1,0:T(2,128)(2,1)S(1)}, u32[]{:S(2)}, u32[]{:S(2)}) %all-to-all-start.2) | async-done | bytes 544 | tf_op jit(solution)/shard_map/while/body/eval_jaxpr/all_to_all | solution.py:63
  25.7 3.3 %all-to-all-start.1 = ((bf16[8,32,128]{2,1,0:T(8,128)(2,1)}), bf16[8,32,128]{2,1,0:T(8,128)(2,1)S(1)}, u32[]{:S(2)}, u32[]{:S(2)}) async-start(bf16[8,32,128]{2,1,0:T(8,128)(2,1)} %copy.49), calls=%async_computation.1 | async-start | bytes 131072 | tf_op jit(solution)/shard_map/while/body/eval_jaxpr/all_to_all | solution.py:62
  29.9 4.8 %all-to-all-done.1 = bf16[8,32,128]{2,1,0:T(8,128)(2,1)S(1)} async-done(((bf16[8,32,128]{2,1,0:T(8,128)(2,1)}), bf16[8,32,128]{2,1,0:T(8,128)(2,1)S(1)}, u32[]{:S(2)}, u32[]{:S(2)}) %all-to-all-start.1) | async-done | bytes 65568 | tf_op jit(solution)/shard_map/while/body/eval_jaxpr/all_to_all | solution.py:62
  34.7 3.3 %all-to-all-start = ((bf16[8,32,128]{2,1,0:T(8,128)(2,1)}), bf16[8,32,128]{2,1,0:T(8,128)(2,1)S(1)}, u32[]{:S(2)}, u32[]{:S(2)}) async-start(bf16[8,32,128]{2,1,0:T(8,128)(2,1)} %convolution_convert_fusion.5), calls=%async_computation | async-start | bytes 131072 | tf_op jit(solution)/shard_map/while/body/eval_jaxpr/all_to_all | solution.py:47
  38.6 1.3 %collective-permute-start.1 = (f32[32,8,128]{2,1,0:T(8,128)S(1)}, f32[32,8,128]{2,1,0:T(8,128)S(1)}, u32[]{:S(2)}, u32[]{:S(2)}) collective-permute-start(f32[32,8,128]{2,1,0:T(8,128)S(1)} %get-tuple-element.676), channel_id=1, source_target_pairs={{2,0},{3,1},{6,4},{7,5},{10,8},{11,9},{14,12},{15,13},{18,16},{19,... | collective-permute-start | bytes 393224 | tf_op jit(solution)/shard_map/while/body/eval_jaxpr/ppermute | solution.py:18
  39.9 3.8 %all-to-all-done = bf16[8,32,128]{2,1,0:T(8,128)(2,1)S(1)} async-done(((bf16[8,32,128]{2,1,0:T(8,128)(2,1)}), bf16[8,32,128]{2,1,0:T(8,128)(2,1)S(1)}, u32[]{:S(2)}, u32[]{:S(2)}) %all-to-all-start) | async-done | bytes 65568 | tf_op jit(solution)/shard_map/while/body/eval_jaxpr/all_to_all | solution.py:47
  43.8 3.4 %collective-permute-start = (f32[32,8,128]{2,1,0:T(8,128)S(1)}, f32[32,8,128]{2,1,0:T(8,128)S(1)}, u32[]{:S(2)}, u32[]{:S(2)}) collective-permute-start(f32[32,8,128]{2,1,0:T(8,128)S(1)} %get-tuple-element.672), channel_id=1, source_target_pairs={{0,2},{1,3},{4,6},{5,7},{8,10},{9,11},{12,14},{13,15},{16,18},{17,... | collective-permute-start | bytes 393224 | tf_op jit(solution)/shard_map/while/body/eval_jaxpr/ppermute | solution.py:18
  47.3 2.5 %collective-permute-done = f32[32,8,128]{2,1,0:T(8,128)S(1)} collective-permute-done((f32[32,8,128]{2,1,0:T(8,128)S(1)}, f32[32,8,128]{2,1,0:T(8,128)S(1)}, u32[]{:S(2)}, u32[]{:S(2)}) %collective-permute-start) | collective-permute-done | bytes 131104 | tf_op jit(solution)/shard_map/while/body/eval_jaxpr/ppermute | solution.py:18
  50.6 3.2 %all-to-all-start.2 = ((bf16[4,2,32]{2,1,0:T(2,128)(2,1)}), bf16[4,2,32]{2,1,0:T(2,128)(2,1)S(1)}, u32[]{:S(2)}, u32[]{:S(2)}) async-start(bf16[4,2,32]{2,1,0:T(2,128)(2,1)} %bitcast.126), calls=%async_computation.2 | async-start | bytes 4096 | tf_op jit(solution)/shard_map/while/body/eval_jaxpr/all_to_all | solution.py:63
  54.9 0.9 convolution_convert_fusion.5
  56.5 2.8 %all-to-all-done.2 = bf16[4,2,32]{2,1,0:T(2,128)(2,1)S(1)} async-done(((bf16[4,2,32]{2,1,0:T(2,128)(2,1)}), bf16[4,2,32]{2,1,0:T(2,128)(2,1)S(1)}, u32[]{:S(2)}, u32[]{:S(2)}) %all-to-all-start.2) | async-done | bytes 544 | tf_op jit(solution)/shard_map/while/body/eval_jaxpr/all_to_all | solution.py:63
  59.3 3.3 %all-to-all-start.1 = ((bf16[8,32,128]{2,1,0:T(8,128)(2,1)}), bf16[8,32,128]{2,1,0:T(8,128)(2,1)S(1)}, u32[]{:S(2)}, u32[]{:S(2)}) async-start(bf16[8,32,128]{2,1,0:T(8,128)(2,1)} %copy.49), calls=%async_computation.1 | async-start | bytes 131072 | tf_op jit(solution)/shard_map/while/body/eval_jaxpr/all_to_all | solution.py:62
  63.5 4.9 %all-to-all-done.1 = bf16[8,32,128]{2,1,0:T(8,128)(2,1)S(1)} async-done(((bf16[8,32,128]{2,1,0:T(8,128)(2,1)}), bf16[8,32,128]{2,1,0:T(8,128)(2,1)S(1)}, u32[]{:S(2)}, u32[]{:S(2)}) %all-to-all-start.1) | async-done | bytes 65568 | tf_op jit(solution)/shard_map/while/body/eval_jaxpr/all_to_all | solution.py:62
  68.5 3.3 %all-to-all-start = ((bf16[8,32,128]{2,1,0:T(8,128)(2,1)}), bf16[8,32,128]{2,1,0:T(8,128)(2,1)S(1)}, u32[]{:S(2)}, u32[]{:S(2)}) async-start(bf16[8,32,128]{2,1,0:T(8,128)(2,1)} %convolution_convert_fusion.5), calls=%async_computation | async-start | bytes 131072 | tf_op jit(solution)/shard_map/while/body/eval_jaxpr/all_to_all | solution.py:47
  72.4 1.3 %collective-permute-start.1 = (f32[32,8,128]{2,1,0:T(8,128)S(1)}, f32[32,8,128]{2,1,0:T(8,128)S(1)}, u32[]{:S(2)}, u32[]{:S(2)}) collective-permute-start(f32[32,8,128]{2,1,0:T(8,128)S(1)} %get-tuple-element.676), channel_id=1, source_target_pairs={{2,0},{3,1},{6,4},{7,5},{10,8},{11,9},{14,12},{15,13},{18,16},{19,... | collective-permute-start | bytes 393224 | tf_op jit(solution)/shard_map/while/body/eval_jaxpr/ppermute | solution.py:18
  73.7 3.8 %all-to-all-done = bf16[8,32,128]{2,1,0:T(8,128)(2,1)S(1)} async-done(((bf16[8,32,128]{2,1,0:T(8,128)(2,1)}), bf16[8,32,128]{2,1,0:T(8,128)(2,1)S(1)}, u32[]{:S(2)}, u32[]{:S(2)}) %all-to-all-start) | async-done | bytes 65568 | tf_op jit(solution)/shard_map/while/body/eval_jaxpr/all_to_all | solution.py:47
  77.6 4.2 %collective-permute-start = (f32[32,8,128]{2,1,0:T(8,128)S(1)}, f32[32,8,128]{2,1,0:T(8,128)S(1)}, u32[]{:S(2)}, u32[]{:S(2)}) collective-permute-start(f32[32,8,128]{2,1,0:T(8,128)S(1)} %get-tuple-element.672), channel_id=1, source_target_pairs={{0,2},{1,3},{4,6},{5,7},{8,10},{9,11},{12,14},{13,15},{16,18},{17,... | collective-permute-start | bytes 393224 | tf_op jit(solution)/shard_map/while/body/eval_jaxpr/ppermute | solution.py:18
  81.9 2.5 %collective-permute-done = f32[32,8,128]{2,1,0:T(8,128)S(1)} collective-permute-done((f32[32,8,128]{2,1,0:T(8,128)S(1)}, f32[32,8,128]{2,1,0:T(8,128)S(1)}, u32[]{:S(2)}, u32[]{:S(2)}) %collective-permute-start) | collective-permute-done | bytes 131104 | tf_op jit(solution)/shard_map/while/body/eval_jaxpr/ppermute | solution.py:18
  85.1 2.5 %psum.7 = f32[1,1024]{1,0:T(1,128)S(1)} all-reduce(f32[1,1024]{1,0:T(1,128)S(1)} %bitcast.139), channel_id=1, replica_groups=mesh['groups'=2,'cells'=4,'tm'=2,'cls'=2] {'cls'}, use_global_device_ids=true, to_apply=%region_5.6 | all-reduce | flops 1024 | bytes 8192 | tf_op jit(solution)/shard_map/psum | solution.py:141
  (85 shorter events, 13.2 us)
Async XLA Ops:
  0.7 1.0 %copy-start.1 = (f32[32,1024]{1,0:T(8,128)S(1)}, f32[32,1024]{1,0:T(8,128)}, u32[]{:S(2)}) copy-start(f32[32,1024]{1,0:T(8,128)} %param.11) | copy-start | bytes 393220
  0.7 1.0 %copy-start.2 = (s32[4]{0:T(128)S(1)}, s32[4]{0:T(128)}, u32[]{:S(2)}) copy-start(s32[4]{0:T(128)} %param.17) | copy-start | bytes 52
  1.7 0.7 copy-start.6
  1.7 13.8 %copy-start = (bf16[8,128,128]{2,1,0:T(8,128)(2,1)S(1)}, bf16[8,128,128]{2,1,0:T(8,128)(2,1)}, u32[]{:S(2)}) copy-start(bf16[8,128,128]{2,1,0:T(8,128)(2,1)} %param.14) | copy-start | bytes 786436
  1.8 0.7 copy-start.4
  1.8 0.7 copy-start.5
  15.4 0.7 copy-start.3
  17.0 8.7 %all-to-all-start.2 = ((bf16[4,2,32]{2,1,0:T(2,128)(2,1)}), bf16[4,2,32]{2,1,0:T(2,128)(2,1)S(1)}, u32[]{:S(2)}, u32[]{:S(2)}) async-start(bf16[4,2,32]{2,1,0:T(2,128)(2,1)} %bitcast.126), calls=%async_computation.2 | async-start | bytes 4096 | tf_op jit(solution)/shard_map/while/body/eval_jaxpr/all_to_all | solution.py:63
  25.7 9.0 %all-to-all-start.1 = ((bf16[8,32,128]{2,1,0:T(8,128)(2,1)}), bf16[8,32,128]{2,1,0:T(8,128)(2,1)S(1)}, u32[]{:S(2)}, u32[]{:S(2)}) async-start(bf16[8,32,128]{2,1,0:T(8,128)(2,1)} %copy.49), calls=%async_computation.1 | async-start | bytes 131072 | tf_op jit(solution)/shard_map/while/body/eval_jaxpr/all_to_all | solution.py:62
  34.7 9.0 %all-to-all-start = ((bf16[8,32,128]{2,1,0:T(8,128)(2,1)}), bf16[8,32,128]{2,1,0:T(8,128)(2,1)S(1)}, u32[]{:S(2)}, u32[]{:S(2)}) async-start(bf16[8,32,128]{2,1,0:T(8,128)(2,1)} %convolution_convert_fusion.5), calls=%async_computation | async-start | bytes 131072 | tf_op jit(solution)/shard_map/while/body/eval_jaxpr/all_to_all | solution.py:47
  38.6 8.7 %collective-permute-start.1 = (f32[32,8,128]{2,1,0:T(8,128)S(1)}, f32[32,8,128]{2,1,0:T(8,128)S(1)}, u32[]{:S(2)}, u32[]{:S(2)}) collective-permute-start(f32[32,8,128]{2,1,0:T(8,128)S(1)} %get-tuple-element.676), channel_id=1, source_target_pairs={{2,0},{3,1},{6,4},{7,5},{10,8},{11,9},{14,12},{15,13},{18,16},{19,... | collective-permute-start | bytes 393224 | tf_op jit(solution)/shard_map/while/body/eval_jaxpr/ppermute | solution.py:18
  43.8 5.9 %collective-permute-start = (f32[32,8,128]{2,1,0:T(8,128)S(1)}, f32[32,8,128]{2,1,0:T(8,128)S(1)}, u32[]{:S(2)}, u32[]{:S(2)}) collective-permute-start(f32[32,8,128]{2,1,0:T(8,128)S(1)} %get-tuple-element.672), channel_id=1, source_target_pairs={{0,2},{1,3},{4,6},{5,7},{8,10},{9,11},{12,14},{13,15},{16,18},{17,... | collective-permute-start | bytes 393224 | tf_op jit(solution)/shard_map/while/body/eval_jaxpr/ppermute | solution.py:18
  50.6 8.7 %all-to-all-start.2 = ((bf16[4,2,32]{2,1,0:T(2,128)(2,1)}), bf16[4,2,32]{2,1,0:T(2,128)(2,1)S(1)}, u32[]{:S(2)}, u32[]{:S(2)}) async-start(bf16[4,2,32]{2,1,0:T(2,128)(2,1)} %bitcast.126), calls=%async_computation.2 | async-start | bytes 4096 | tf_op jit(solution)/shard_map/while/body/eval_jaxpr/all_to_all | solution.py:63
  59.3 9.2 %all-to-all-start.1 = ((bf16[8,32,128]{2,1,0:T(8,128)(2,1)}), bf16[8,32,128]{2,1,0:T(8,128)(2,1)S(1)}, u32[]{:S(2)}, u32[]{:S(2)}) async-start(bf16[8,32,128]{2,1,0:T(8,128)(2,1)} %copy.49), calls=%async_computation.1 | async-start | bytes 131072 | tf_op jit(solution)/shard_map/while/body/eval_jaxpr/all_to_all | solution.py:62
  68.5 9.0 %all-to-all-start = ((bf16[8,32,128]{2,1,0:T(8,128)(2,1)}), bf16[8,32,128]{2,1,0:T(8,128)(2,1)S(1)}, u32[]{:S(2)}, u32[]{:S(2)}) async-start(bf16[8,32,128]{2,1,0:T(8,128)(2,1)} %convolution_convert_fusion.5), calls=%async_computation | async-start | bytes 131072 | tf_op jit(solution)/shard_map/while/body/eval_jaxpr/all_to_all | solution.py:47
  72.4 9.5 %collective-permute-start.1 = (f32[32,8,128]{2,1,0:T(8,128)S(1)}, f32[32,8,128]{2,1,0:T(8,128)S(1)}, u32[]{:S(2)}, u32[]{:S(2)}) collective-permute-start(f32[32,8,128]{2,1,0:T(8,128)S(1)} %get-tuple-element.676), channel_id=1, source_target_pairs={{2,0},{3,1},{6,4},{7,5},{10,8},{11,9},{14,12},{15,13},{18,16},{19,... | collective-permute-start | bytes 393224 | tf_op jit(solution)/shard_map/while/body/eval_jaxpr/ppermute | solution.py:18
  77.6 6.8 %collective-permute-start = (f32[32,8,128]{2,1,0:T(8,128)S(1)}, f32[32,8,128]{2,1,0:T(8,128)S(1)}, u32[]{:S(2)}, u32[]{:S(2)}) collective-permute-start(f32[32,8,128]{2,1,0:T(8,128)S(1)} %get-tuple-element.672), channel_id=1, source_target_pairs={{0,2},{1,3},{4,6},{5,7},{8,10},{9,11},{12,14},{13,15},{16,18},{17,... | collective-permute-start | bytes 393224 | tf_op jit(solution)/shard_map/while/body/eval_jaxpr/ppermute | solution.py:18
where the time goes:
time: 89.8 us; the launch traced here: 88.9 us
  starting transfers between devices  29.8 us (33%)
  waiting for transfers between devices  27.9 us (31%)
  blocking collectives  14.1 us (16%)
  local copies, waits for them, and re-layouts  8.44 us (9%)
  matrix products  5.26 us (6%)
  other arithmetic  2.18 us (2%)
    all_to_all x1, blocking collectives, shards(): lax.all_to_all(target_block, 'cells', split_axis=0, concat_axis=0, tiled=...  11.7 us
    ppermute x4, starting transfers between devices, from_behind(): return lax.ppermute(shard, axis, pairs)  10.2 us
    all_to_all x2, waiting for transfers between devices, retreat(): lax.all_to_all(sent_weight, 'cells', split_axis=0, concat_axis=0, tiled=T...  9.68 us
    all_to_all x2, waiting for transfers between devices, advance(): lax.all_to_all(partial_value, 'cells', split_axis=0, concat_axis=0, tiled...  7.6 us
    all_to_all x2, starting transfers between devices, advance(): lax.all_to_all(partial_value, 'cells', split_axis=0, concat_axis=0, tiled...  6.57 us
    all_to_all x2, starting transfers between devices, retreat(): lax.all_to_all(sent_weight, 'cells', split_axis=0, concat_axis=0, tiled=T...  6.57 us
    all_to_all x2, starting transfers between devices, retreat(): lax.all_to_all(sent_low, 'cells', split_axis=0, concat_axis=0, tiled=True)  6.45 us
    all_to_all x2, waiting for transfers between devices, retreat(): lax.all_to_all(sent_low, 'cells', split_axis=0, concat_axis=0, tiled=True)  5.68 us
  transfers between devices with their start and end apart: 10, of which 8 were waited for; matrix products, arithmetic and copies ran while one was open for 9% of the time, Pallas kernels for 0%

commit v1 on v0

v1 whole, which is shorter than its diff:
```python
import functools

import jax
import jax.numpy as jnp
from jax import lax
from jax.experimental import pallas as pl
from jax.experimental.pallas import tpu as pltpu
from jax.sharding import PartitionSpec as P

BS = 128
CLASSES = 64

base_cost = 0.05
far_below = -1e30
MESH = pl.DeviceIdType.MESH


def loop(low, high, body, carry):
    if high - low <= 8:
        for index in range(low, high):
            carry = body(index, carry)
        return carry
    return lax.fori_loop(low, high, body, carry)


def kernel(
    sizes, src_s, dst_s, len_s, start_hbm, final_hbm, cong_hbm, cap_hbm, trans_hbm,
    dens_out, mean_out, val_out,
    masses, values, cong, cap, trans, moving, weight, ceiling, edge_log, sums,
    dst_send, dst_recv, part_send, part_recv, back_send, back_recv, class_sums,
    in_sem, dst_ssem, dst_rsem, part_ssem, part_rsem, back_ssem, back_rsem,
    cong_ssem, cong_rsem, mean_ssem, mean_rsem,
):
    owners, sections, halves, per_peer, local_steps, block_count, class_count = sizes
    steps = sections * local_steps
    me = lax.axis_index("cells")
    section = lax.axis_index("tm")
    half = lax.axis_index("cls")
    columns = [slice(b * BS, (b + 1) * BS) for b in range(block_count)]

    def after(axis, size, by):
        return {axis: lax.rem(lax.axis_index(axis) + by, size)}

    barrier = pltpu.get_barrier_semaphore()
    greeted = 0
    for axis, size in (("cells", owners), ("tm", sections), ("cls", halves)):

        def greet(by, carry, axis=axis, size=size):
            pl.semaphore_signal(
                barrier, inc=1, device_id=after(axis, size, by), device_id_type=MESH
            )
            return carry

        loop(1, size, greet, 0)
        greeted += size - 1

    own_cong = cong.at[section]
    loads = [
        pltpu.make_async_copy(cong_hbm, own_cong, in_sem.at[0]),
        pltpu.make_async_copy(cap_hbm, cap, in_sem.at[1]),
        pltpu.make_async_copy(final_hbm, values, in_sem.at[2]),
        pltpu.make_async_copy(start_hbm, masses, in_sem.at[3]),
        pltpu.make_async_copy(trans_hbm, trans, in_sem.at[4]),
    ]
    for load in loads:
        load.start()

    def target_rows(by, carry):
        peer = lax.rem(me + by, owners)
        for s in range(per_peer):
            target = jnp.where(s < len_s[peer], dst_s[peer * per_peer + s], -1)
            dst_send[by, s : s + 1, :] = jnp.full((1, BS), target, jnp.int32)
        return carry

    loop(0, owners, target_rows, 0)
    dst_recv[0] = dst_send[0]
    pl.semaphore_wait(barrier, greeted)

    def dst_copy(by):
        return pltpu.make_async_remote_copy(
            src_ref=dst_send.at[by], dst_ref=dst_recv.at[by],
            send_sem=dst_ssem.at[by], recv_sem=dst_rsem.at[by],
            device_id=after("cells", owners, by), device_id_type=MESH,
        )

    def cong_copy(by):
        return pltpu.make_async_remote_copy(
            src_ref=cong_hbm, dst_ref=cong.at[section],
            send_sem=cong_ssem.at[by], recv_sem=cong_rsem.at[section],
            device_id=after("tm", sections, by), device_id_type=MESH,
        )

    def cong_arrival(owner):
        return pltpu.make_async_remote_copy(
            src_ref=cong_hbm, dst_ref=cong.at[owner],
            send_sem=cong_ssem.at[0], recv_sem=cong_rsem.at[owner],
            device_id=after("tm", sections, 1), device_id_type=MESH,
        )

    def part_copy(r, by):
        return pltpu.make_async_remote_copy(
            src_ref=part_send.at[r, by], dst_ref=part_recv.at[r, by],
            send_sem=part_ssem.at[r, by], recv_sem=part_rsem.at[r, by],
            device_id=after("cells", owners, by), device_id_type=MESH,
        )

    def back_copy(r, by):
        return pltpu.make_async_remote_copy(
            src_ref=back_send.at[r, by], dst_ref=back_recv.at[r, by],
            send_sem=back_ssem.at[r, by], recv_sem=back_rsem.at[r, by],
            device_id=after("cells", owners, owners - by), device_id_type=MESH,
        )

    def mean_copy(by):
        return pltpu.make_async_remote_copy(
            src_ref=class_sums.at[0], dst_ref=class_sums.at[by],
            send_sem=mean_ssem.at[by], recv_sem=mean_rsem.at[by],
            device_id=after("cls", halves, by), device_id_type=MESH,
        )

    def started(copy):
        def body(by, carry):
            copy(by).start()
            return carry

        return body

    def sent(copy):
        def body(by, carry):
            copy(by).wait_send()
            return carry

        return body

    loop(1, sections, started(cong_copy), 0)
    loop(1, owners, started(dst_copy), 0)

    def one_loading(step, b):
        owner, local = divmod(step, local_steps)
        return cong[owner, local : local + 1, columns[b]] / cap[:, columns[b]]

    def forward_send(r):
        owner, local = divmod(r, local_steps)
        if owner < sections - 1 and local == 0:

            @pl.when(section > owner)
            def _():
                cong_arrival(owner).wait_recv()

        for b in range(block_count):
            mobility = 1.0 / (1.0 + one_loading(r, b))
            now = masses[:, columns[b]]
            moving[b] = (now * mobility).astype(jnp.bfloat16)
            masses[:, columns[b]] = now * (1.0 - mobility)

        def one_peer(by, carry):
            peer = lax.rem(me + by, owners)
            into = part_recv if isinstance(by, int) and by == 0 else part_send
            for s in range(per_peer):
                e = peer * per_peer + s
                into[r, by, s] = jnp.dot(
                    moving[src_s[e]], trans[e], preferred_element_type=jnp.float32
                ).astype(jnp.bfloat16)
            if into is part_send:
                part_copy(r, by).start()
            return carry

        loop(1, owners, one_peer, 0)
        one_peer(0, 0)

    def forward_receive(r):
        owner, local = divmod(r, local_steps)

        def one_source(by, totals):
            if not (isinstance(by, int) and by == 0):
                part_copy(r, by).wait_recv()
            totals = list(totals)
            for s in range(per_peer):
                row = jnp.broadcast_to(dst_recv[by, s : s + 1, :], (class_count, BS))
                part = part_recv[r, by, s].astype(jnp.float32)
                for b in range(block_count):
                    totals[b] = totals[b] + jnp.where(row == b, part, 0.0)
            return tuple(totals)

        totals = one_source(0, tuple(masses[:, c] for c in columns))
        totals = loop(1, owners, one_source, totals)
        for b in range(block_count):
            masses[:, columns[b]] = totals[b]

        @pl.when(section == owner)
        def _():
            for b in range(block_count):
                total = masses[:, columns[b]]
                dens_out[local, :, columns[b]] = total
                class_sums[0, local : local + 1, columns[b]] = jnp.sum(
                    total, axis=0, keepdims=True
                )
            if local == local_steps - 1:
                loop(1, halves, started(mean_copy), 0)

    def backward_send(r):
        lane = lax.broadcasted_iota(jnp.int32, (class_count, BS), 1)
        lows = jnp.zeros((class_count, BS), jnp.float32)
        for b in range(block_count):
            now = values[:, columns[b]]
            low = jnp.min(now, axis=1, keepdims=True)
            low = low.astype(jnp.bfloat16).astype(jnp.float32)
            weight[b] = jnp.exp(low - now)
            lows = jnp.where(lane == b, low, lows)
        lows = lows.astype(jnp.bfloat16)

        def one_source(by, carry):
            here = isinstance(by, int) and by == 0
            into = back_recv if here else back_send
            if r == 0 and not here:
                dst_copy(by).wait_recv()
            for s in range(per_peer):
                row = jnp.broadcast_to(dst_recv[by, s : s + 1, :], (class_count, BS))
                picked = jnp.zeros((class_count, BS), jnp.float32)
                for b in range(block_count):
                    picked = jnp.where(row == b, weight[b], picked)
                into[r, by, s] = picked.astype(jnp.bfloat16)
            into[r, by, per_peer] = lows
            if not here:
                back_copy(r, by).start()
            return carry

        loop(1, owners, one_source, 0)
        one_source(0, 0)

    def backward_receive(r):
        step = steps - 1 - r
        owner, local = divmod(step, local_steps)
        lane = lax.broadcasted_iota(jnp.int32, (class_count, BS), 1)

        def one_peer(by, tops):
            if not (isinstance(by, int) and by == 0):
                back_copy(r, by).wait_recv()
            peer = lax.rem(me + by, owners)
            tops = list(tops)
            lows = back_recv[r, by, per_peer].astype(jnp.float32)
            for s in range(per_peer):
                e = peer * per_peer + s
                low = jnp.sum(jnp.where(lane == dst_s[e], lows, 0.0), axis=1, keepdims=True)
                log = jnp.where(s < len_s[peer], -low, far_below)
                log = jnp.broadcast_to(log, (class_count, BS))
                edge_log[by * per_peer + s] = log
                sums[by * per_peer + s] = lax.dot_general(
                    back_recv[r, by, s], trans[e], (((1,), (1,)), ((), ())),
                    preferred_element_type=jnp.float32,
                )
                for b in range(block_count):
                    tops[b] = jnp.maximum(tops[b], jnp.where(src_s[e] == b, log, far_below))
            return tuple(tops)

        tops = one_peer(0, tuple(-values[:, c] for c in columns))
        tops = loop(1, owners, one_peer, tops)
        for b in range(block_count):
            ceiling[b] = tops[b]

        def one_total(by, totals):
            peer = lax.rem(me + by, owners)
            totals = list(totals)
            for s in range(per_peer):
                source = src_s[peer * per_peer + s]
                place = by * per_peer + s
                term = jnp.exp(edge_log[place] - ceiling[source]) * sums[place]
                for b in range(block_count):
                    totals[b] = totals[b] + jnp.where(source == b, term, 0.0)
            return tuple(totals)

        if owner > 0 and local == local_steps - 1:

            @pl.when(section < owner)
            def _():
                cong_arrival(owner).wait_recv()

        totals = tuple(jnp.exp(-values[:, columns[b]] - ceiling[b]) for b in range(block_count))
        totals = loop(0, owners, one_total, totals)
        for b in range(block_count):
            travel = base_cost * (1.0 + one_loading(step, b))
            values[:, columns[b]] = travel - (ceiling[b] + jnp.log(totals[b]))

        @pl.when(section == owner)
        def _():
            val_out[local] = values[...]

    for load in loads:
        load.wait()

    def forward_guard(r, body):
        owner = r // local_steps
        if owner == 0:
            body(r)
        else:

            @pl.when(section >= owner)
            def _():
                body(r)


    def backward_guard(r, body):
        owner = (steps - 1 - r) // local_steps
        if owner == sections - 1:
            body(r)
        else:

            @pl.when(section <= owner)
            def _():
                body(r)


    forward_guard(0, forward_send)
    backward_guard(0, backward_send)
    for r in range(steps):
        forward_guard(r, forward_receive)
        if r + 1 < steps:
            forward_guard(r + 1, forward_send)
        backward_guard(r, backward_receive)
        if r + 1 < steps:
            backward_guard(r + 1, backward_send)

    def arrived(by, carry):
        mean_copy(by).wait_recv()
        return carry

    loop(1, halves, arrived, 0)
    total = class_sums[half]
    for index in range(1, halves):
        total = total + class_sums[lax.rem(half - index + halves, halves)]
    mean_out[...] = total / CLASSES

    loop(1, sections, sent(cong_copy), 0)
    loop(1, owners, sent(dst_copy), 0)
    loop(1, halves, sent(mean_copy), 0)
    for r in range(steps):
        forward_guard(r, lambda r: loop(1, owners, sent(functools.partial(part_copy, r)), 0))
        backward_guard(r, lambda r: loop(1, owners, sent(functools.partial(back_copy, r)), 0))


def shards(
    start_density, final_value, congestion, capacity, trans_values, src_local, dst_local, bucket_len
):
    owners = lax.axis_size("cells")
    sections = lax.axis_size("tm")
    halves = lax.axis_size("cls")
    class_count, cell_count = start_density.shape
    local_steps = congestion.shape[0]
    block_count = cell_count // BS
    edge_count = src_local.shape[0]
    per_peer = edge_count // owners
    steps = sections * local_steps
    sizes = (owners, sections, halves, per_peer, local_steps, block_count, class_count)
    scalars = pl.BlockSpec(memory_space=pltpu.SMEM)
    whole = pl.BlockSpec(memory_space=pl.ANY)
    held = pl.BlockSpec(memory_space=pltpu.VMEM)
    f32, bf16 = jnp.float32, jnp.bfloat16
    tile = (class_count, BS)
    return pl.pallas_call(
        functools.partial(kernel, sizes),
        out_shape=(
            jax.ShapeDtypeStruct((local_steps, class_count, cell_count), f32),
            jax.ShapeDtypeStruct((local_steps, cell_count), f32),
            jax.ShapeDtypeStruct((local_steps, class_count, cell_count), f32),
        ),
        in_specs=[scalars] * 3 + [whole] * 5,
        out_specs=(held, held, held),
        scratch_shapes=[
            pltpu.VMEM((class_count, cell_count), f32),
            pltpu.VMEM((class_count, cell_count), f32),
            pltpu.VMEM((sections, local_steps, cell_count), f32),
            pltpu.VMEM((1, cell_count), f32),
            pltpu.VMEM((edge_count, BS, BS), bf16),
            pltpu.VMEM((block_count, *tile), bf16),
            pltpu.VMEM((block_count, *tile), f32),
            pltpu.VMEM((block_count, *tile), f32),
            pltpu.VMEM((edge_count, *tile), f32),
            pltpu.VMEM((edge_count, *tile), f32),
            pltpu.VMEM((owners, per_peer, BS), jnp.int32),
            pltpu.VMEM((owners, per_peer, BS), jnp.int32),
            pltpu.VMEM((steps, owners, per_peer, *tile), bf16),
            pltpu.VMEM((steps, owners, per_peer, *tile), bf16),
            pltpu.VMEM((steps, owners, per_peer + 1, *tile), bf16),
            pltpu.VMEM((steps, owners, per_peer + 1, *tile), bf16),
            pltpu.VMEM((halves, local_steps, cell_count), f32),
            pltpu.SemaphoreType.DMA((5,)),
            pltpu.SemaphoreType.DMA((owners,)),
            pltpu.SemaphoreType.DMA((owners,)),
            pltpu.SemaphoreType.DMA((steps, owners)),
            pltpu.SemaphoreType.DMA((steps, owners)),
            pltpu.SemaphoreType.DMA((steps, owners)),
            pltpu.SemaphoreType.DMA((steps, owners)),
            pltpu.SemaphoreType.DMA((sections,)),
            pltpu.SemaphoreType.DMA((sections,)),
            pltpu.SemaphoreType.DMA((halves,)),
            pltpu.SemaphoreType.DMA((halves,)),
        ],
        compiler_params=pltpu.CompilerParams(
            collective_id=0, has_side_effects=True, vmem_limit_bytes=40 * 1024 * 1024
        ),
    )(
        src_local, dst_local, bucket_len, start_density, final_value, congestion,
        capacity.reshape(1, cell_count), trans_values,
    )


def solution(mesh):
    in_specs = (
        P(("groups", "cls"), "cells"),
        P(("groups", "cls"), "cells"),
        P(("groups", "tm"), "cells"),
        P(("groups", "cells")),
        P(("groups", "cells"), None, None),
        P(("groups", "cells")),
        P(("groups", "cells")),
        P(("groups", "cells")),
    )
    out_specs = (
        P(("groups", "tm"), "cls", "cells"),
        P(("groups", "tm"), "cells"),
        P(("groups", "tm"), "cls", "cells"),
    )
    return jax.shard_map(shards, mesh=mesh, in_specs=in_specs, out_specs=out_specs, check_vma=False)
```

time: 89.8 us -> 25.9 us (0.29)
  starting transfers between devices: 29.8 us -> 0 us
  waiting for transfers between devices: 27.9 us -> 0 us
  Pallas kernels: 0 us -> 18.2 us
  blocking collectives: 14.1 us -> 0 us
  matrix products: 5.26 us -> 0 us
  other arithmetic: 2.18 us -> 0 us
  local copies, waits for them, and re-layouts: 8.44 us -> 6.7 us
    all_to_all x6 -> x0, waiting for transfers between devices: 23 us -> none  [the longest x2 9.68 us: retreat(): lax.all_to_all(sent_weight, 'cells', split_axis=0, concat_axis=0, tiled=T...]
    all_to_all x6 -> x0, starting transfers between devices: 19.6 us -> none  [the longest x2 6.57 us: advance(): lax.all_to_all(partial_value, 'cells', split_axis=0, concat_axis=0, tiled...]
    pallas_call x0 -> x1, Pallas kernels: none -> 18.2 us  [shards(): pl.pallas_call(functools.partial(kernel, sizes), out_shape=(jax.ShapeDtyp...]
    all_to_all x1 -> x0, blocking collectives: 11.7 us -> none  [shards(): lax.all_to_all(target_block, 'cells', split_axis=0, concat_axis=0, tiled=...]
    ppermute x4 -> x0, starting transfers between devices: 10.2 us -> none  [from_behind(): return lax.ppermute(shard, axis, pairs)]
    dot_general x12 -> x0, matrix products: 5.26 us -> none  [the longest x2 1.75 us: advance(): jnp.einsum('ceb,ebk->eck', picked, trans_values, preferred_element_type=j...]
    ppermute x4 -> x0, waiting for transfers between devices: 4.97 us -> none  [from_behind(): return lax.ppermute(shard, axis, pairs)]
    unnamed x16 -> x19, local copies, waits for them, and re-layouts: 2.16 us -> 6.7 us
  transfers between devices with their start and end apart: 10 -> 0, of which waited for: 8 -> 0; matrix products, arithmetic and copies ran while one was open for 9% -> 0% of each run, Pallas kernels for 0% -> 0%
where the time goes in v1:
time: 25.9 us; the launch traced here: 25.6 us
  Pallas kernels  18.2 us (70%)
  local copies, waits for them, and re-layouts  6.7 us (26%)
  between operations  0.67 us (3%)
    pallas_call x1, Pallas kernels, shards(): pl.pallas_call(functools.partial(kernel, sizes), out_shape=(jax.ShapeDtyp...  18.2 us
    unnamed x19, local copies, waits for them, and re-layouts  6.7 us

profile of v1, /device:TPU:0, one launch (start us, length us, event | category | flops | bytes accessed | tf_op | source)
XLA Modules:
  0.0 25.6 jit_solution(6472169860131827649)
XLA Ops:
  0.6 0.0 copy-start.7
  0.6 0.0 copy-start.6
  0.7 0.0 copy-start.5
  0.7 0.6 %copy-done.7 = s32[4]{0:T(128)S(1)} copy-done((s32[4]{0:T(128)S(1)}, s32[4]{0:T(128)}, u32[]{:S(2)}) %copy-start.7) | copy-done | bytes 40
  1.3 0.0 copy-done.6
  1.3 0.0 copy-done.5
  1.3 0.0 copy-start
  1.3 0.9 %copy-done = bf16[8,128,128]{2,1,0:T(8,128)(2,1)S(1)} copy-done((bf16[8,128,128]{2,1,0:T(8,128)(2,1)S(1)}, bf16[8,128,128]{2,1,0:T(8,128)(2,1)}, u32[]{:S(2)}) %copy-start) | copy-done | bytes 262168
  2.3 0.0 copy-start.1
  2.3 0.9 %copy-done.1 = f32[32,1024]{1,0:T(8,128)S(1)} copy-done((f32[32,1024]{1,0:T(8,128)S(1)}, f32[32,1024]{1,0:T(8,128)}, u32[]{:S(2)}) %copy-start.1) | copy-done | bytes 131096
  3.2 0.0 copy-start.2
  3.2 0.9 %copy-done.2 = f32[32,1024]{1,0:T(8,128)S(1)} copy-done((f32[32,1024]{1,0:T(8,128)S(1)}, f32[32,1024]{1,0:T(8,128)}, u32[]{:S(2)}) %copy-start.2) | copy-done | bytes 131096
  4.1 0.0 copy-start.3
  4.1 0.7 %copy-done.3 = f32[1,1024]{1,0:T(1,128)S(1)} copy-done((f32[1,1024]{1,0:T(1,128)S(1)}, f32[1,1024]{1,0:T(1,128)}, u32[]{:S(2)}) %copy-start.3) | copy-done | bytes 4120
  4.8 0.0 copy-start.4
  4.8 0.7 %copy-done.4 = f32[1024]{0:T(1024)S(1)} copy-done((f32[1024]{0:T(1024)S(1)}, f32[1024]{0:T(1024)}, u32[]{:S(2)}) %copy-start.4) | copy-done | bytes 4120
  5.5 18.2 %shard_map.103 = (f32[1,32,1024]{2,1,0:T(8,128)S(1)}, f32[1,1024]{1,0:T(1,128)S(1)}, f32[1,32,1024]{2,1,0:T(8,128)S(1)}) custom-call(s32[8]{0:T(128)S(1)} %copy-done.5, s32[8]{0:T(128)S(1)} %copy-done.6, s32[4]{0:T(128)S(1)} %copy-done.7, f32[32,1024]{1,0:T(8,128)S(1)} %copy-done.1, f32[32,1024]{1,0:T(8,128)S(1)} %copy-done.2, f32[1,1024]{1,0:T(1,128)S(1)} %copy-done.3, ...), custom_call_target="tpu_custom_call" | custom-call | tf_op jit(solution)/shard_map/pallas_call | solution.py:359
  23.7 0.7 %copy.14 = f32[1,32,1024]{2,1,0:T(8,128)} copy(f32[1,32,1024]{2,1,0:T(8,128)S(1)} %get-tuple-element.6) | data formatting | bytes 262144
  24.3 0.6 %copy.15 = f32[1,1024]{1,0:T(1,128)} copy(f32[1,1024]{1,0:T(1,128)S(1)} %get-tuple-element.7) | data formatting | bytes 8192
  24.9 0.7 %copy.16 = f32[1,32,1024]{2,1,0:T(8,128)} copy(f32[1,32,1024]{2,1,0:T(8,128)S(1)} %get-tuple-element.8) | data formatting | bytes 262144
Async XLA Ops:
  0.6 0.7 %copy-start.7 = (s32[4]{0:T(128)S(1)}, s32[4]{0:T(128)}, u32[]{:S(2)}) copy-start(s32[4]{0:T(128)} %len_s.1) | copy-start | bytes 52
  0.6 0.7 %copy-start.6 = (s32[8]{0:T(128)S(1)}, s32[8]{0:T(128)}, u32[]{:S(2)}) copy-start(s32[8]{0:T(128)} %dst_s.1) | copy-start | bytes 100
  0.7 0.7 %copy-start.5 = (s32[8]{0:T(128)S(1)}, s32[8]{0:T(128)}, u32[]{:S(2)}) copy-start(s32[8]{0:T(128)} %src_s.1) | copy-start | bytes 100
  1.3 0.9 %copy-start = (bf16[8,128,128]{2,1,0:T(8,128)(2,1)S(1)}, bf16[8,128,128]{2,1,0:T(8,128)(2,1)}, u32[]{:S(2)}) copy-start(bf16[8,128,128]{2,1,0:T(8,128)(2,1)} %trans_hbm.1) | copy-start | bytes 786436
  2.3 0.9 %copy-start.1 = (f32[32,1024]{1,0:T(8,128)S(1)}, f32[32,1024]{1,0:T(8,128)}, u32[]{:S(2)}) copy-start(f32[32,1024]{1,0:T(8,128)} %start_hbm.1) | copy-start | bytes 393220
  3.2 0.9 %copy-start.2 = (f32[32,1024]{1,0:T(8,128)S(1)}, f32[32,1024]{1,0:T(8,128)}, u32[]{:S(2)}) copy-start(f32[32,1024]{1,0:T(8,128)} %final_hbm.1) | copy-start | bytes 393220
  4.1 0.7 %copy-start.3 = (f32[1,1024]{1,0:T(1,128)S(1)}, f32[1,1024]{1,0:T(1,128)}, u32[]{:S(2)}) copy-start(f32[1,1024]{1,0:T(1,128)} %cong_hbm.1) | copy-start | bytes 12292
  4.8 0.7 %copy-start.4 = (f32[1024]{0:T(1024)S(1)}, f32[1024]{0:T(1024)}, u32[]{:S(2)}) copy-start(f32[1024]{0:T(1024)} %param.11) | copy-start | bytes 12292

commit v2 on v1

--- a/solution.py
+++ b/solution.py
@@ -12,6 +12,8 @@
 
 base_cost = 0.05
 far_below = -1e30
+VMEM_BYTES = 64 * 1024 * 1024
+VMEM_SPARE = 256 * 1024
 MESH = pl.DeviceIdType.MESH
 
 
@@ -24,8 +26,9 @@
 
 
 def kernel(
-    sizes, src_s, dst_s, len_s, start_hbm, final_hbm, cong_hbm, cap_hbm, trans_hbm,
-    dens_out, mean_out, val_out,
+    sizes, src_hbm, dst_hbm, len_hbm, start_hbm, final_hbm, cong_hbm, cap_hbm, trans_hbm,
+    dens_hbm, mean_hbm, val_hbm,
+    dens_out, mean_out, val_out, out_sem, src_s, dst_s, len_s,
     masses, values, cong, cap, trans, moving, weight, ceiling, edge_log, sums,
     dst_send, dst_recv, part_send, part_recv, back_send, back_recv, class_sums,
     in_sem, dst_ssem, dst_rsem, part_ssem, part_rsem, back_ssem, back_rsem,
@@ -54,7 +57,15 @@
         loop(1, size, greet, 0)
         greeted += size - 1
 
+    dens_store = pltpu.make_async_copy(dens_out, dens_hbm, out_sem.at[0])
+    val_store = pltpu.make_async_copy(val_out, val_hbm, out_sem.at[1])
+    mean_store = pltpu.make_async_copy(mean_out, mean_hbm, out_sem.at[2])
     own_cong = cong.at[section]
+    scalar_loads = [
+        pltpu.make_async_copy(src_hbm, src_s, in_sem.at[5]),
+        pltpu.make_async_copy(dst_hbm, dst_s, in_sem.at[6]),
+        pltpu.make_async_copy(len_hbm, len_s, in_sem.at[7]),
+    ]
     loads = [
         pltpu.make_async_copy(cong_hbm, own_cong, in_sem.at[0]),
         pltpu.make_async_copy(cap_hbm, cap, in_sem.at[1]),
@@ -62,8 +73,10 @@
         pltpu.make_async_copy(start_hbm, masses, in_sem.at[3]),
         pltpu.make_async_copy(trans_hbm, trans, in_sem.at[4]),
     ]
-    for load in loads:
+    for load in scalar_loads + loads:
         load.start()
+    for load in scalar_loads:
+        load.wait()
 
     def target_rows(by, carry):
         peer = lax.rem(me + by, owners)
@@ -197,6 +210,7 @@
                 )
             if local == local_steps - 1:
                 loop(1, halves, started(mean_copy), 0)
+                dens_store.start()
 
     def backward_send(r):
         lane = lax.broadcasted_iota(jnp.int32, (class_count, BS), 1)
@@ -283,7 +297,10 @@
 
         @pl.when(section == owner)
         def _():
-            val_out[local] = values[...]
+            for b in range(block_count):
+                val_out[local, :, columns[b]] = values[:, columns[b]]
+            if local == 0:
+                val_store.start()
 
     for load in loads:
         load.wait()
@@ -329,6 +346,7 @@
     for index in range(1, halves):
         total = total + class_sums[lax.rem(half - index + halves, halves)]
     mean_out[...] = total / CLASSES
+    mean_store.start()
 
     loop(1, sections, sent(cong_copy), 0)
     loop(1, owners, sent(dst_copy), 0)
@@ -336,6 +354,21 @@
     for r in range(steps):
         forward_guard(r, lambda r: loop(1, owners, sent(functools.partial(part_copy, r)), 0))
         backward_guard(r, lambda r: loop(1, owners, sent(functools.partial(back_copy, r)), 0))
+    dens_store.wait()
+    val_store.wait()
+    mean_store.wait()
+
+
+def write_out(dens_in, mean_in, val_in, dens_out, mean_out, val_out, sem):
+    copies = [
+        pltpu.make_async_copy(dens_in, dens_out, sem.at[0]),
+        pltpu.make_async_copy(val_in, val_out, sem.at[1]),
+        pltpu.make_async_copy(mean_in, mean_out, sem.at[2]),
+    ]
+    for copy in copies:
+        copy.start()
+    for copy in copies:
+        copy.wait()
 
 
 def shards(
@@ -351,21 +384,28 @@
     per_peer = edge_count // owners
     steps = sections * local_steps
     sizes = (owners, sections, halves, per_peer, local_steps, block_count, class_count)
-    scalars = pl.BlockSpec(memory_space=pltpu.SMEM)
+    far = pl.BlockSpec(memory_space=pltpu.HBM)
     whole = pl.BlockSpec(memory_space=pl.ANY)
-    held = pl.BlockSpec(memory_space=pltpu.VMEM)
     f32, bf16 = jnp.float32, jnp.bfloat16
     tile = (class_count, BS)
-    return pl.pallas_call(
+    results = (
+        jax.ShapeDtypeStruct((local_steps, class_count, cell_count), f32),
+        jax.ShapeDtypeStruct((local_steps, cell_count), f32),
+        jax.ShapeDtypeStruct((local_steps, class_count, cell_count), f32),
+    )
+    computed = pl.pallas_call(
         functools.partial(kernel, sizes),
-        out_shape=(
-            jax.ShapeDtypeStruct((local_steps, class_count, cell_count), f32),
-            jax.ShapeDtypeStruct((local_steps, cell_count), f32),
-            jax.ShapeDtypeStruct((local_steps, class_count, cell_count), f32),
-        ),
-        in_specs=[scalars] * 3 + [whole] * 5,
-        out_specs=(held, held, held),
+        out_shape=results,
+        in_specs=[far] * 8,
+        out_specs=(whole, whole, whole),
         scratch_shapes=[
+            pltpu.VMEM((local_steps, class_count, cell_count), f32),
+            pltpu.VMEM((local_steps, cell_count), f32),
+            pltpu.VMEM((local_steps, class_count, cell_count), f32),
+            pltpu.SemaphoreType.DMA((3,)),
+            pltpu.SMEM((edge_count,), jnp.int32),
+            pltpu.SMEM((edge_count,), jnp.int32),
+            pltpu.SMEM((owners,), jnp.int32),
             pltpu.VMEM((class_count, cell_count), f32),
             pltpu.VMEM((class_count, cell_count), f32),
             pltpu.VMEM((sections, local_steps, cell_count), f32),
@@ -383,7 +423,7 @@
             pltpu.VMEM((steps, owners, per_peer + 1, *tile), bf16),
             pltpu.VMEM((steps, owners, per_peer + 1, *tile), bf16),
             pltpu.VMEM((halves, local_steps, cell_count), f32),
-            pltpu.SemaphoreType.DMA((5,)),
+            pltpu.SemaphoreType.DMA((8,)),
             pltpu.SemaphoreType.DMA((owners,)),
             pltpu.SemaphoreType.DMA((owners,)),
             pltpu.SemaphoreType.DMA((steps, owners)),
@@ -396,12 +436,20 @@
             pltpu.SemaphoreType.DMA((halves,)),
         ],
         compiler_params=pltpu.CompilerParams(
-            collective_id=0, has_side_effects=True, vmem_limit_bytes=40 * 1024 * 1024
+            collective_id=0, has_side_effects=True, vmem_limit_bytes=VMEM_BYTES - VMEM_SPARE
         ),
     )(
         src_local, dst_local, bucket_len, start_density, final_value, congestion,
         capacity.reshape(1, cell_count), trans_values,
     )
+    return pl.pallas_call(
+        write_out,
+        out_shape=results,
+        in_specs=[whole] * 3,
+        out_specs=[whole] * 3,
+        scratch_shapes=[pltpu.SemaphoreType.DMA((3,))],
+        compiler_params=pltpu.CompilerParams(vmem_limit_bytes=VMEM_BYTES - VMEM_SPARE),
+    )(*computed)
 
 
 def solution(mesh):

time: 25.9 us -> 28.4 us (1.097)
  Pallas kernels: 18.2 us -> 27.5 us
  local copies, waits for them, and re-layouts: 6.7 us -> 0 us
    pallas_call x1 -> x2, Pallas kernels: 18.2 us -> 27.5 us  [the longest x1 18.4 us: shards(): pl.pallas_call(functools.partial(kernel, sizes), out_shape=results, in_sp...]
    unnamed x19 -> x0, local copies, waits for them, and re-layouts: 6.7 us -> none
where the time goes in v2:
time: 28.4 us; the launch traced here: 28.2 us
  Pallas kernels  27.5 us (97%)
  between operations  0.64 us (2%)
    pallas_call x1, Pallas kernels, shards(): pl.pallas_call(functools.partial(kernel, sizes), out_shape=results, in_sp...  18.4 us
    pallas_call x1, Pallas kernels, shards(): pl.pallas_call(write_out, out_shape=results, in_specs=[whole] * 3, out_sp...  9.2 us

profile of v2, /device:TPU:0, one launch (start us, length us, event | category | flops | bytes accessed | tf_op | source)
XLA Modules:
  0.0 28.2 jit_solution(4241576731463968747)
XLA Ops:
  0.6 18.4 %shard_map.103 = (f32[1,32,1024]{2,1,0:T(8,128)}, f32[1,1024]{1,0:T(1,128)}, f32[1,32,1024]{2,1,0:T(8,128)}) custom-call(s32[8]{0:T(128)} %src_hbm.1, s32[8]{0:T(128)} %dst_hbm.1, s32[4]{0:T(128)} %len_hbm.1, f32[32,1024]{1,0:T(8,128)} %start_hbm.1, f32[32,1024]{1,0:T(8,128)} %final_hbm.1, f32[1,1024]{1,0:T(1,128)} %cong_hbm.1, f32[1,1024]{1,0:T(1,128)} %bitcast.1, ...), custom_call_target="tpu_custom_call" | custom-call | tf_op jit(solution)/shard_map/pallas_call | solution.py:396
  19.0 9.2 %shard_map.104 = (f32[1,32,1024]{2,1,0:T(8,128)}, f32[1,1024]{1,0:T(1,128)}, f32[1,32,1024]{2,1,0:T(8,128)}) custom-call(f32[1,32,1024]{2,1,0:T(8,128)} %get-tuple-element.6.dens_in, f32[1,1024]{1,0:T(1,128)} %get-tuple-element.7.mean_in, f32[1,32,1024]{2,1,0:T(8,128)} %get-tuple-element.8.val_in), custom_call_target="tpu_custom_call" | custom-call | tf_op jit(solution)/shard_map/pallas_call | solution.py:445

commit v3 on v2

--- a/solution.py
+++ b/solution.py
@@ -12,8 +12,7 @@
 
 base_cost = 0.05
 far_below = -1e30
-VMEM_BYTES = 64 * 1024 * 1024
-VMEM_SPARE = 256 * 1024
+KERNEL_BYTES = 32 * 1024 * 1024
 MESH = pl.DeviceIdType.MESH
 
 
@@ -27,8 +26,8 @@
 
 def kernel(
     sizes, src_hbm, dst_hbm, len_hbm, start_hbm, final_hbm, cong_hbm, cap_hbm, trans_hbm,
-    dens_hbm, mean_hbm, val_hbm,
-    dens_out, mean_out, val_out, out_sem, src_s, dst_s, len_s,
+    dens_out, mean_out, val_out,
+    src_s, dst_s, len_s,
     masses, values, cong, cap, trans, moving, weight, ceiling, edge_log, sums,
     dst_send, dst_recv, part_send, part_recv, back_send, back_recv, class_sums,
     in_sem, dst_ssem, dst_rsem, part_ssem, part_rsem, back_ssem, back_rsem,
@@ -57,9 +56,6 @@
         loop(1, size, greet, 0)
         greeted += size - 1
 
-    dens_store = pltpu.make_async_copy(dens_out, dens_hbm, out_sem.at[0])
-    val_store = pltpu.make_async_copy(val_out, val_hbm, out_sem.at[1])
-    mean_store = pltpu.make_async_copy(mean_out, mean_hbm, out_sem.at[2])
     own_cong = cong.at[section]
     scalar_loads = [
         pltpu.make_async_copy(src_hbm, src_s, in_sem.at[5]),
@@ -210,7 +206,6 @@
                 )
             if local == local_steps - 1:
                 loop(1, halves, started(mean_copy), 0)
-                dens_store.start()
 
     def backward_send(r):
         lane = lax.broadcasted_iota(jnp.int32, (class_count, BS), 1)
@@ -299,8 +294,6 @@
         def _():
             for b in range(block_count):
                 val_out[local, :, columns[b]] = values[:, columns[b]]
-            if local == 0:
-                val_store.start()
 
     for load in loads:
         load.wait()
@@ -346,7 +339,6 @@
     for index in range(1, halves):
         total = total + class_sums[lax.rem(half - index + halves, halves)]
     mean_out[...] = total / CLASSES
-    mean_store.start()
 
     loop(1, sections, sent(cong_copy), 0)
     loop(1, owners, sent(dst_copy), 0)
@@ -354,9 +346,6 @@
     for r in range(steps):
         forward_guard(r, lambda r: loop(1, owners, sent(functools.partial(part_copy, r)), 0))
         backward_guard(r, lambda r: loop(1, owners, sent(functools.partial(back_copy, r)), 0))
-    dens_store.wait()
-    val_store.wait()
-    mean_store.wait()
 
 
 def write_out(dens_in, mean_in, val_in, dens_out, mean_out, val_out, sem):
@@ -384,6 +373,7 @@
     per_peer = edge_count // owners
     steps = sections * local_steps
     sizes = (owners, sections, halves, per_peer, local_steps, block_count, class_count)
+    held = pl.BlockSpec(memory_space=pltpu.VMEM)
     far = pl.BlockSpec(memory_space=pltpu.HBM)
     whole = pl.BlockSpec(memory_space=pl.ANY)
     f32, bf16 = jnp.float32, jnp.bfloat16
@@ -395,14 +385,10 @@
     )
     computed = pl.pallas_call(
         functools.partial(kernel, sizes),
-        out_shape=results,
+        out_shape=tuple(pltpu.VMEM(r.shape, r.dtype) for r in results),
         in_specs=[far] * 8,
-        out_specs=(whole, whole, whole),
+        out_specs=(held, held, held),
         scratch_shapes=[
-            pltpu.VMEM((local_steps, class_count, cell_count), f32),
-            pltpu.VMEM((local_steps, cell_count), f32),
-            pltpu.VMEM((local_steps, class_count, cell_count), f32),
-            pltpu.SemaphoreType.DMA((3,)),
             pltpu.SMEM((edge_count,), jnp.int32),
             pltpu.SMEM((edge_count,), jnp.int32),
             pltpu.SMEM((owners,), jnp.int32),
@@ -436,19 +422,21 @@
             pltpu.SemaphoreType.DMA((halves,)),
         ],
         compiler_params=pltpu.CompilerParams(
-            collective_id=0, has_side_effects=True, vmem_limit_bytes=VMEM_BYTES - VMEM_SPARE
+            collective_id=0, has_side_effects=True, vmem_limit_bytes=KERNEL_BYTES
         ),
-    )(
-        src_local, dst_local, bucket_len, start_density, final_value, congestion,
-        capacity.reshape(1, cell_count), trans_values,
-    )
+    )(*(
+        pltpu.with_memory_space_constraint(operand, pltpu.HBM)
+        for operand in (
+            src_local, dst_local, bucket_len, start_density, final_value, congestion,
+            capacity.reshape(1, cell_count), trans_values,
+        )
+    ))
     return pl.pallas_call(
         write_out,
         out_shape=results,
         in_specs=[whole] * 3,
         out_specs=[whole] * 3,
         scratch_shapes=[pltpu.SemaphoreType.DMA((3,))],
-        compiler_params=pltpu.CompilerParams(vmem_limit_bytes=VMEM_BYTES - VMEM_SPARE),
     )(*computed)
 
 

time: 28.4 us -> 29.6 us (1.042)
  local copies, waits for them, and re-layouts: 0 us -> 1.86 us
  Pallas kernels: 27.5 us -> 26.9 us
    unnamed x0 -> x6, local copies, waits for them, and re-layouts: none -> 1.86 us
    pallas_call x1, Pallas kernels: 18.4 us -> 17.7 us  [shards(): pl.pallas_call(functools.partial(kernel, sizes), out_shape=tuple((pltpu.V...]
where the time goes in v3:
time: 29.6 us; the launch traced here: 29.4 us
  Pallas kernels  26.9 us (91%)
  local copies, waits for them, and re-layouts  1.86 us (6%)
  between operations  0.65 us (2%)
    pallas_call x1, Pallas kernels, shards(): pl.pallas_call(functools.partial(kernel, sizes), out_shape=tuple((pltpu.V...  17.7 us
    pallas_call x1, Pallas kernels, shards(): pl.pallas_call(write_out, out_shape=results, in_specs=[whole] * 3, out_sp...  9.19 us
    unnamed x6, local copies, waits for them, and re-layouts  1.86 us

profile of v3, /device:TPU:0, one launch (start us, length us, event | category | flops | bytes accessed | tf_op | source)
XLA Modules:
  0.0 29.4 jit_solution(4476765195110514213)
XLA Ops:
  0.6 17.7 %shard_map.103 = (f32[1,32,1024]{2,1,0:T(8,128)S(1)}, f32[1,1024]{1,0:T(1,128)S(1)}, f32[1,32,1024]{2,1,0:T(8,128)S(1)}) custom-call(s32[8]{0:T(128)} %src_hbm.1, s32[8]{0:T(128)} %dst_hbm.1, s32[4]{0:T(128)} %len_hbm.1, f32[32,1024]{1,0:T(8,128)} %start_hbm.1, f32[32,1024]{1,0:T(8,128)} %final_hbm.1, f32[1,1024]{1,0:T(1,128)} %cong_hbm.1, ...), custom_call_target="tpu_custom_call" | custom-call | tf_op jit(solution)/shard_map/pallas_call | solution.py:386
  18.4 0.0 copy-start
  18.4 0.6 %copy-done = f32[1,32,1024]{2,1,0:T(8,128)} copy-done((f32[1,32,1024]{2,1,0:T(8,128)}, f32[1,32,1024]{2,1,0:T(8,128)S(1)}, u32[]{:S(2)}) %copy-start) | copy-done | bytes 131096
  19.0 0.0 copy-start.1
  19.0 0.6 %copy-done.1 = f32[1,32,1024]{2,1,0:T(8,128)} copy-done((f32[1,32,1024]{2,1,0:T(8,128)}, f32[1,32,1024]{2,1,0:T(8,128)S(1)}, u32[]{:S(2)}) %copy-start.1) | copy-done | bytes 131096
  19.6 0.0 copy-start.2
  19.6 0.6 %copy-done.2 = f32[1,1024]{1,0:T(1,128)} copy-done((f32[1,1024]{1,0:T(1,128)}, f32[1,1024]{1,0:T(1,128)S(1)}, u32[]{:S(2)}) %copy-start.2) | copy-done | bytes 4120
  20.2 9.2 %shard_map.104 = (f32[1,32,1024]{2,1,0:T(8,128)}, f32[1,1024]{1,0:T(1,128)}, f32[1,32,1024]{2,1,0:T(8,128)}) custom-call(f32[1,32,1024]{2,1,0:T(8,128)} %copy-done, f32[1,1024]{1,0:T(1,128)} %copy-done.2, f32[1,32,1024]{2,1,0:T(8,128)} %copy-done.1), custom_call_target="tpu_custom_call" | custom-call | tf_op jit(solution)/shard_map/pallas_call | solution.py:434
Async XLA Ops:
  18.4 0.6 %copy-start = (f32[1,32,1024]{2,1,0:T(8,128)}, f32[1,32,1024]{2,1,0:T(8,128)S(1)}, u32[]{:S(2)}) copy-start(f32[1,32,1024]{2,1,0:T(8,128)S(1)} %get-tuple-element.6.dens_in) | copy-start | bytes 393220
  19.0 0.6 %copy-start.1 = (f32[1,32,1024]{2,1,0:T(8,128)}, f32[1,32,1024]{2,1,0:T(8,128)S(1)}, u32[]{:S(2)}) copy-start(f32[1,32,1024]{2,1,0:T(8,128)S(1)} %get-tuple-element.8.val_in) | copy-start | bytes 393220
  19.6 0.6 %copy-start.2 = (f32[1,1024]{1,0:T(1,128)}, f32[1,1024]{1,0:T(1,128)S(1)}, u32[]{:S(2)}) copy-start(f32[1,1024]{1,0:T(1,128)S(1)} %get-tuple-element.7.mean_in) | copy-start | bytes 12292

commit v4 on v3

--- a/solution.py
+++ b/solution.py
@@ -12,6 +12,7 @@
 
 base_cost = 0.05
 far_below = -1e30
+LOW_ROWS = 16
 KERNEL_BYTES = 32 * 1024 * 1024
 MESH = pl.DeviceIdType.MESH
 
@@ -38,6 +39,7 @@
     me = lax.axis_index("cells")
     section = lax.axis_index("tm")
     half = lax.axis_index("cls")
+    groups = class_count // LOW_ROWS
     columns = [slice(b * BS, (b + 1) * BS) for b in range(block_count)]
 
     def after(axis, size, by):
@@ -208,14 +210,16 @@
                 loop(1, halves, started(mean_copy), 0)
 
     def backward_send(r):
-        lane = lax.broadcasted_iota(jnp.int32, (class_count, BS), 1)
-        lows = jnp.zeros((class_count, BS), jnp.float32)
+        lane = lax.broadcasted_iota(jnp.int32, (LOW_ROWS, BS), 1)
+        lows = jnp.zeros((LOW_ROWS, BS), jnp.float32)
         for b in range(block_count):
             now = values[:, columns[b]]
             low = jnp.min(now, axis=1, keepdims=True)
             low = low.astype(jnp.bfloat16).astype(jnp.float32)
             weight[b] = jnp.exp(low - now)
-            lows = jnp.where(lane == b, low, lows)
+            for g in range(groups):
+                part = low[g * LOW_ROWS : (g + 1) * LOW_ROWS]
+                lows = jnp.where(lane == g * block_count + b, part, lows)
         lows = lows.astype(jnp.bfloat16)
 
         def one_source(by, carry):
@@ -228,8 +232,8 @@
                 picked = jnp.zeros((class_count, BS), jnp.float32)
                 for b in range(block_count):
                     picked = jnp.where(row == b, weight[b], picked)
-                into[r, by, s] = picked.astype(jnp.bfloat16)
-            into[r, by, per_peer] = lows
+                into[r, by, s * class_count : (s + 1) * class_count] = picked.astype(jnp.bfloat16)
+            into[r, by, per_peer * class_count :] = lows
             if not here:
                 back_copy(r, by).start()
             return carry
@@ -240,22 +244,32 @@
     def backward_receive(r):
         step = steps - 1 - r
         owner, local = divmod(step, local_steps)
-        lane = lax.broadcasted_iota(jnp.int32, (class_count, BS), 1)
+        lane = lax.broadcasted_iota(jnp.int32, (LOW_ROWS, BS), 1)
 
         def one_peer(by, tops):
             if not (isinstance(by, int) and by == 0):
                 back_copy(r, by).wait_recv()
             peer = lax.rem(me + by, owners)
             tops = list(tops)
-            lows = back_recv[r, by, per_peer].astype(jnp.float32)
+            lows = back_recv[r, by, per_peer * class_count :].astype(jnp.float32)
             for s in range(per_peer):
                 e = peer * per_peer + s
-                low = jnp.sum(jnp.where(lane == dst_s[e], lows, 0.0), axis=1, keepdims=True)
+                low = jnp.concatenate(
+                    [
+                        jnp.sum(
+                            jnp.where(lane == g * block_count + dst_s[e], lows, 0.0),
+                            axis=1,
+                            keepdims=True,
+                        )
+                        for g in range(groups)
+                    ],
+                    axis=0,
+                )
                 log = jnp.where(s < len_s[peer], -low, far_below)
                 log = jnp.broadcast_to(log, (class_count, BS))
                 edge_log[by * per_peer + s] = log
                 sums[by * per_peer + s] = lax.dot_general(
-                    back_recv[r, by, s], trans[e], (((1,), (1,)), ((), ())),
+                    back_recv[r, by, s * class_count : (s + 1) * class_count], trans[e], (((1,), (1,)), ((), ())),
                     preferred_element_type=jnp.float32,
                 )
                 for b in range(block_count):
@@ -406,8 +420,8 @@
             pltpu.VMEM((owners, per_peer, BS), jnp.int32),
             pltpu.VMEM((steps, owners, per_peer, *tile), bf16),
             pltpu.VMEM((steps, owners, per_peer, *tile), bf16),
-            pltpu.VMEM((steps, owners, per_peer + 1, *tile), bf16),
-            pltpu.VMEM((steps, owners, per_peer + 1, *tile), bf16),
+            pltpu.VMEM((steps, owners, per_peer * class_count + LOW_ROWS, BS), bf16),
+            pltpu.VMEM((steps, owners, per_peer * class_count + LOW_ROWS, BS), bf16),
             pltpu.VMEM((halves, local_steps, cell_count), f32),
             pltpu.SemaphoreType.DMA((8,)),
             pltpu.SemaphoreType.DMA((owners,)),
@@ -437,7 +451,8 @@
         in_specs=[whole] * 3,
         out_specs=[whole] * 3,
         scratch_shapes=[pltpu.SemaphoreType.DMA((3,))],
-    )(*computed)
+        compiler_params=pltpu.CompilerParams(vmem_limit_bytes=1024 * 1024),
+    )(*(pltpu.with_memory_space_constraint(part, pltpu.VMEM) for part in computed))
 
 
 def solution(mesh):

time: 29.6 us -> 19.2 us (0.65)
  Pallas kernels: 26.9 us -> 18.4 us
  local copies, waits for them, and re-layouts: 1.86 us -> 0 us
    pallas_call x1, Pallas kernels: 9.19 us -> 0.73 us  [shards(): pl.pallas_call(write_out, out_shape=results, in_specs=[whole] * 3, out_sp...]
    unnamed x6 -> x0, local copies, waits for them, and re-layouts: 1.86 us -> none
where the time goes in v4:
time: 19.2 us; the launch traced here: 19.1 us
  Pallas kernels  18.4 us (96%)
  between operations  0.64 us (3%)
    pallas_call x1, Pallas kernels, shards(): pl.pallas_call(functools.partial(kernel, sizes), out_shape=tuple((pltpu.V...  17.7 us
    pallas_call x1, Pallas kernels, shards(): pl.pallas_call(write_out, out_shape=results, in_specs=[whole] * 3, out_sp...  0.73 us

profile of v4, /device:TPU:0, one launch (start us, length us, event | category | flops | bytes accessed | tf_op | source)
XLA Modules:
  0.0 19.1 jit_solution(7835763314123758370)
XLA Ops:
  0.6 17.7 %shard_map.103 = (f32[1,32,1024]{2,1,0:T(8,128)S(1)}, f32[1,1024]{1,0:T(1,128)S(1)}, f32[1,32,1024]{2,1,0:T(8,128)S(1)}) custom-call(s32[8]{0:T(128)} %src_hbm.1, s32[8]{0:T(128)} %dst_hbm.1, s32[4]{0:T(128)} %len_hbm.1, f32[32,1024]{1,0:T(8,128)} %start_hbm.1, f32[32,1024]{1,0:T(8,128)} %final_hbm.1, f32[1,1024]{1,0:T(1,128)} %cong_hbm.1, ...), custom_call_target="tpu_custom_call" | custom-call | tf_op jit(solution)/shard_map/pallas_call | solution.py:400
  18.3 0.7 %shard_map.104 = (f32[1,32,1024]{2,1,0:T(8,128)}, f32[1,1024]{1,0:T(1,128)}, f32[1,32,1024]{2,1,0:T(8,128)}) custom-call(f32[1,32,1024]{2,1,0:T(8,128)S(1)} %get-tuple-element.6.dens_in, f32[1,1024]{1,0:T(1,128)S(1)} %get-tuple-element.7.mean_in, f32[1,32,1024]{2,1,0:T(8,128)S(1)} %get-tuple-element.8.val_in), custom_call_target="tpu_custom_call" | custom-call | tf_op jit(solution)/shard_map/pallas_call | solution.py:448

commit v5 on v4

--- a/solution.py
+++ b/solution.py
@@ -29,10 +29,11 @@
     sizes, src_hbm, dst_hbm, len_hbm, start_hbm, final_hbm, cong_hbm, cap_hbm, trans_hbm,
     dens_out, mean_out, val_out,
     src_s, dst_s, len_s,
-    masses, values, cong, cap, trans, moving, weight, ceiling, edge_log, sums,
-    dst_send, dst_recv, part_send, part_recv, back_send, back_recv, class_sums,
+    start, final, density, value, stay, cong, cap, trans, moving, weight, ceiling, edge_log, sums,
+    dst_send, dst_recv, part_send, part_recv, back_send, back_recv, sums_send, class_sums,
     in_sem, dst_ssem, dst_rsem, part_ssem, part_rsem, back_ssem, back_rsem,
     cong_ssem, cong_rsem, mean_ssem, mean_rsem,
+    dens_ssem, dens_rsem, val_ssem, val_rsem,
 ):
     owners, sections, halves, per_peer, local_steps, block_count, class_count = sizes
     steps = sections * local_steps
@@ -46,17 +47,27 @@
         return {axis: lax.rem(lax.axis_index(axis) + by, size)}
 
     barrier = pltpu.get_barrier_semaphore()
-    greeted = 0
-    for axis, size in (("cells", owners), ("tm", sections), ("cls", halves)):
-
-        def greet(by, carry, axis=axis, size=size):
-            pl.semaphore_signal(
-                barrier, inc=1, device_id=after(axis, size, by), device_id_type=MESH
-            )
-            return carry
-
-        loop(1, size, greet, 0)
-        greeted += size - 1
+    def greet(by, carry):
+        pl.semaphore_signal(
+            barrier, inc=1, device_id=after("cells", owners, by), device_id_type=MESH
+        )
+        return carry
+
+    def greet_beside(by, carry):
+        pl.semaphore_signal(
+            barrier,
+            inc=1,
+            device_id={
+                "tm": lax.rem(section + by // halves, sections),
+                "cls": lax.rem(half + by % halves, halves),
+            },
+            device_id_type=MESH,
+        )
+        return carry
+
+    loop(1, owners, greet, 0)
+    loop(1, sections * halves, greet_beside, 0)
+    greeted = owners - 1 + sections * halves - 1
 
     own_cong = cong.at[section]
     scalar_loads = [
@@ -67,8 +78,8 @@
     loads = [
         pltpu.make_async_copy(cong_hbm, own_cong, in_sem.at[0]),
         pltpu.make_async_copy(cap_hbm, cap, in_sem.at[1]),
-        pltpu.make_async_copy(final_hbm, values, in_sem.at[2]),
-        pltpu.make_async_copy(start_hbm, masses, in_sem.at[3]),
+        pltpu.make_async_copy(final_hbm, final, in_sem.at[2]),
+        pltpu.make_async_copy(start_hbm, start, in_sem.at[3]),
         pltpu.make_async_copy(trans_hbm, trans, in_sem.at[4]),
     ]
     for load in scalar_loads + loads:
@@ -94,18 +105,42 @@
             device_id=after("cells", owners, by), device_id_type=MESH,
         )
 
-    def cong_copy(by):
+    def cong_copy(target):
         return pltpu.make_async_remote_copy(
             src_ref=cong_hbm, dst_ref=cong.at[section],
-            send_sem=cong_ssem.at[by], recv_sem=cong_rsem.at[section],
-            device_id=after("tm", sections, by), device_id_type=MESH,
+            send_sem=cong_ssem.at[target], recv_sem=cong_rsem.at[section],
+            device_id={"tm": target}, device_id_type=MESH,
         )
 
     def cong_arrival(owner):
         return pltpu.make_async_remote_copy(
             src_ref=cong_hbm, dst_ref=cong.at[owner],
             send_sem=cong_ssem.at[0], recv_sem=cong_rsem.at[owner],
-            device_id=after("tm", sections, 1), device_id_type=MESH,
+            device_id={"tm": lax.rem(section + 1, sections)}, device_id_type=MESH,
+        )
+
+    def dens_copy(step):
+        owner, local = divmod(step, local_steps)
+        return pltpu.make_async_remote_copy(
+            src_ref=density.at[step], dst_ref=dens_out.at[local],
+            send_sem=dens_ssem.at[step], recv_sem=dens_rsem.at[local],
+            device_id={"tm": owner}, device_id_type=MESH,
+        )
+
+    def val_copy(step):
+        owner, local = divmod(step, local_steps)
+        return pltpu.make_async_remote_copy(
+            src_ref=value.at[step], dst_ref=val_out.at[local],
+            send_sem=val_ssem.at[step], recv_sem=val_rsem.at[local],
+            device_id={"tm": owner}, device_id_type=MESH,
+        )
+
+    def mean_copy(step, by):
+        owner, local = divmod(step, local_steps)
+        return pltpu.make_async_remote_copy(
+            src_ref=sums_send.at[step], dst_ref=class_sums.at[half, local],
+            send_sem=mean_ssem.at[step, by], recv_sem=mean_rsem.at[half, local],
+            device_id={"tm": owner, "cls": lax.rem(half + by, halves)}, device_id_type=MESH,
         )
 
     def part_copy(r, by):
@@ -120,13 +155,6 @@
             src_ref=back_send.at[r, by], dst_ref=back_recv.at[r, by],
             send_sem=back_ssem.at[r, by], recv_sem=back_rsem.at[r, by],
             device_id=after("cells", owners, owners - by), device_id_type=MESH,
-        )
-
-    def mean_copy(by):
-        return pltpu.make_async_remote_copy(
-            src_ref=class_sums.at[0], dst_ref=class_sums.at[by],
-            send_sem=mean_ssem.at[by], recv_sem=mean_rsem.at[by],
-            device_id=after("cls", halves, by), device_id_type=MESH,
         )
 
     def started(copy):
@@ -143,8 +171,14 @@
 
         return body
 
-    loop(1, sections, started(cong_copy), 0)
     loop(1, owners, started(dst_copy), 0)
+    ends = sorted({0, sections - 1}) if sections > 1 else []
+    for target in ends:
+
+        @pl.when(section != target)
+        def _(target=target):
+            cong_copy(target).start()
+
 
     def one_loading(step, b):
         owner, local = divmod(step, local_steps)
@@ -153,16 +187,13 @@
     def forward_send(r):
         owner, local = divmod(r, local_steps)
         if owner < sections - 1 and local == 0:
-
-            @pl.when(section > owner)
-            def _():
-                cong_arrival(owner).wait_recv()
-
+            cong_arrival(owner).wait_recv()
+        masses = start if r == 0 else density.at[r - 1]
         for b in range(block_count):
             mobility = 1.0 / (1.0 + one_loading(r, b))
             now = masses[:, columns[b]]
             moving[b] = (now * mobility).astype(jnp.bfloat16)
-            masses[:, columns[b]] = now * (1.0 - mobility)
+            stay[:, columns[b]] = now * (1.0 - mobility)
 
         def one_peer(by, carry):
             peer = lax.rem(me + by, owners)
@@ -184,6 +215,8 @@
 
         def one_source(by, totals):
             if not (isinstance(by, int) and by == 0):
+                if r == 0 and sections > 1:
+                    dst_copy(by).wait_recv()
                 part_copy(r, by).wait_recv()
             totals = list(totals)
             for s in range(per_peer):
@@ -193,23 +226,23 @@
                     totals[b] = totals[b] + jnp.where(row == b, part, 0.0)
             return tuple(totals)
 
-        totals = one_source(0, tuple(masses[:, c] for c in columns))
+        totals = one_source(0, tuple(stay[:, c] for c in columns))
         totals = loop(1, owners, one_source, totals)
         for b in range(block_count):
-            masses[:, columns[b]] = totals[b]
-
-        @pl.when(section == owner)
-        def _():
-            for b in range(block_count):
-                total = masses[:, columns[b]]
-                dens_out[local, :, columns[b]] = total
-                class_sums[0, local : local + 1, columns[b]] = jnp.sum(
-                    total, axis=0, keepdims=True
-                )
-            if local == local_steps - 1:
-                loop(1, halves, started(mean_copy), 0)
+            if owner == sections - 1:
+                dens_out[local, :, columns[b]] = totals[b]
+            if r + 1 < steps:
+                density[r, :, columns[b]] = totals[b]
+        if owner < sections - 1:
+            dens_copy(r).start()
+        for b in range(block_count):
+            sums_send[r, :, columns[b]] = jnp.sum(totals[b], axis=0, keepdims=True)
+        if owner == sections - 1:
+            class_sums[half, local] = sums_send[r]
+        loop(int(owner == sections - 1), halves, started(functools.partial(mean_copy, r)), 0)
 
     def backward_send(r):
+        values = final if r == 0 else value.at[steps - r]
         lane = lax.broadcasted_iota(jnp.int32, (LOW_ROWS, BS), 1)
         lows = jnp.zeros((LOW_ROWS, BS), jnp.float32)
         for b in range(block_count):
@@ -244,6 +277,7 @@
     def backward_receive(r):
         step = steps - 1 - r
         owner, local = divmod(step, local_steps)
+        values = final if r == 0 else value.at[step + 1]
         lane = lax.broadcasted_iota(jnp.int32, (LOW_ROWS, BS), 1)
 
         def one_peer(by, tops):
@@ -293,73 +327,98 @@
             return tuple(totals)
 
         if owner > 0 and local == local_steps - 1:
-
-            @pl.when(section < owner)
-            def _():
-                cong_arrival(owner).wait_recv()
+            cong_arrival(owner).wait_recv()
 
         totals = tuple(jnp.exp(-values[:, columns[b]] - ceiling[b]) for b in range(block_count))
         totals = loop(0, owners, one_total, totals)
         for b in range(block_count):
             travel = base_cost * (1.0 + one_loading(step, b))
-            values[:, columns[b]] = travel - (ceiling[b] + jnp.log(totals[b]))
-
-        @pl.when(section == owner)
-        def _():
-            for b in range(block_count):
-                val_out[local, :, columns[b]] = values[:, columns[b]]
+            result = travel - (ceiling[b] + jnp.log(totals[b]))
+            if owner == 0:
+                val_out[local, :, columns[b]] = result
+            if step > 0:
+                value[step, :, columns[b]] = result
+        if owner > 0:
+            val_copy(step).start()
 
     for load in loads:
         load.wait()
 
-    def forward_guard(r, body):
-        owner = r // local_steps
-        if owner == 0:
-            body(r)
-        else:
-
-            @pl.when(section >= owner)
-            def _():
-                body(r)
-
-
-    def backward_guard(r, body):
-        owner = (steps - 1 - r) // local_steps
-        if owner == sections - 1:
-            body(r)
-        else:
-
-            @pl.when(section <= owner)
-            def _():
-                body(r)
-
-
-    forward_guard(0, forward_send)
-    backward_guard(0, backward_send)
-    for r in range(steps):
-        forward_guard(r, forward_receive)
-        if r + 1 < steps:
-            forward_guard(r + 1, forward_send)
-        backward_guard(r, backward_receive)
-        if r + 1 < steps:
-            backward_guard(r + 1, backward_send)
-
-    def arrived(by, carry):
-        mean_copy(by).wait_recv()
+    @pl.when(section == sections - 1)
+    def _():
+        for r in range(steps):
+            forward_send(r)
+            forward_receive(r)
+
+    @pl.when(section == 0)
+    def _():
+        for r in range(steps):
+            backward_send(r)
+            backward_receive(r)
+
+    def dst_arrived(by, carry):
+        dst_copy(by).wait_recv()
         return carry
 
-    loop(1, halves, arrived, 0)
-    total = class_sums[half]
-    for index in range(1, halves):
-        total = total + class_sums[lax.rem(half - index + halves, halves)]
-    mean_out[...] = total / CLASSES
-
-    loop(1, sections, sent(cong_copy), 0)
+    if sections > 2:
+
+        @pl.when((section > 0) & (section < sections - 1))
+        def _():
+            loop(1, owners, dst_arrived, 0)
+
+    for local in range(local_steps):
+
+        def arrived(source, carry, local=local):
+            pltpu.make_async_remote_copy(
+                src_ref=sums_send.at[local], dst_ref=class_sums.at[source, local],
+                send_sem=mean_ssem.at[0, 0], recv_sem=mean_rsem.at[source, local],
+                device_id=after("cls", halves, 1), device_id_type=MESH,
+            ).wait_recv()
+            return carry
+
+        def arrived_beside(by, carry, arrived=arrived):
+            return arrived(lax.rem(half + by, halves), carry)
+
+        loop(1, halves, arrived_beside, 0)
+        if sections > 1:
+
+            @pl.when(section != sections - 1)
+            def _(arrived=arrived, local=local):
+                arrived(half, 0)
+                dens_copy(local).wait_recv()
+
+            @pl.when(section != 0)
+            def _(local=local):
+                val_copy(steps - local_steps + local).wait_recv()
+
+        total = class_sums[0, local]
+        for index in range(1, halves):
+            total = total + class_sums[index, local]
+        mean_out[local : local + 1, :] = total / CLASSES
+
     loop(1, owners, sent(dst_copy), 0)
-    loop(1, halves, sent(mean_copy), 0)
-    for r in range(steps):
-        forward_guard(r, lambda r: loop(1, owners, sent(functools.partial(part_copy, r)), 0))
-        backward_guard(r, lambda r: loop(1, owners, sent(functools.partial(back_copy, r)), 0))
+    for target in ends:
+
+        @pl.when(section != target)
+        def _(target=target):
+            cong_copy(target).wait_send()
+
+    @pl.when(section == sections - 1)
+    def _():
+        for r in range(steps):
+            owner = r // local_steps
+            loop(1, owners, sent(functools.partial(part_copy, r)), 0)
+            loop(int(owner == sections - 1), halves, sent(functools.partial(mean_copy, r)), 0)
+            if owner < sections - 1:
+                dens_copy(r).wait_send()
+
+    @pl.when(section == 0)
+    def _():
+        for r in range(steps):
+            step = steps - 1 - r
+            loop(1, owners, sent(functools.partial(back_copy, r)), 0)
+            if step // local_steps > 0:
+                val_copy(step).wait_send()
 
 
 def write_out(dens_in, mean_in, val_in, dens_out, mean_out, val_out, sem):
@@ -408,6 +467,9 @@
             pltpu.SMEM((owners,), jnp.int32),
             pltpu.VMEM((class_count, cell_count), f32),
             pltpu.VMEM((class_count, cell_count), f32),
+            pltpu.VMEM((steps, class_count, cell_count), f32),
+            pltpu.VMEM((steps, class_count, cell_count), f32),
+            pltpu.VMEM((class_count, cell_count), f32),
             pltpu.VMEM((sections, local_steps, cell_count), f32),
             pltpu.VMEM((1, cell_count), f32),
             pltpu.VMEM((edge_count, BS, BS), bf16),
@@ -422,7 +484,8 @@
             pltpu.VMEM((steps, owners, per_peer, *tile), bf16),
             pltpu.VMEM((steps, owners, per_peer * class_count + LOW_ROWS, BS), bf16),
             pltpu.VMEM((steps, owners, per_peer * class_count + LOW_ROWS, BS), bf16),
-            pltpu.VMEM((halves, local_steps, cell_count), f32),
+            pltpu.VMEM((steps, 1, cell_count), f32),
+            pltpu.VMEM((halves, local_steps, 1, cell_count), f32),
             pltpu.SemaphoreType.DMA((8,)),
             pltpu.SemaphoreType.DMA((owners,)),
             pltpu.SemaphoreType.DMA((owners,)),
@@ -432,8 +495,12 @@
             pltpu.SemaphoreType.DMA((steps, owners)),
             pltpu.SemaphoreType.DMA((sections,)),
             pltpu.SemaphoreType.DMA((sections,)),
-            pltpu.SemaphoreType.DMA((halves,)),
-            pltpu.SemaphoreType.DMA((halves,)),
+            pltpu.SemaphoreType.DMA((steps, halves)),
+            pltpu.SemaphoreType.DMA((halves, local_steps)),
+            pltpu.SemaphoreType.DMA((steps,)),
+            pltpu.SemaphoreType.DMA((local_steps,)),
+            pltpu.SemaphoreType.DMA((steps,)),
+            pltpu.SemaphoreType.DMA((local_steps,)),
         ],
         compiler_params=pltpu.CompilerParams(
             collective_id=0, has_side_effects=True, vmem_limit_bytes=KERNEL_BYTES

time: 19.2 us -> 19.3 us (level)
  no operation moved by 1% of the time
where the time goes in v5:
time: 19.3 us; the launch traced here: 19.1 us
  Pallas kernels  18.5 us (96%)
  between operations  0.64 us (3%)
    pallas_call x1, Pallas kernels, shards(): pl.pallas_call(functools.partial(kernel, sizes), out_shape=tuple((pltpu.V...  17.8 us
    pallas_call x1, Pallas kernels, shards(): pl.pallas_call(write_out, out_shape=results, in_specs=[whole] * 3, out_sp...  0.73 us

profile of v5, /device:TPU:0, one launch (start us, length us, event | category | flops | bytes accessed | tf_op | source)
XLA Modules:
  0.0 19.1 jit_solution(3861787956692154202)
XLA Ops:
  0.6 17.8 %shard_map.103 = (f32[1,32,1024]{2,1,0:T(8,128)S(1)}, f32[1,1024]{1,0:T(1,128)S(1)}, f32[1,32,1024]{2,1,0:T(8,128)S(1)}) custom-call(s32[8]{0:T(128)} %src_hbm.1, s32[8]{0:T(128)} %dst_hbm.1, s32[4]{0:T(128)} %len_hbm.1, f32[32,1024]{1,0:T(8,128)} %start_hbm.1, f32[32,1024]{1,0:T(8,128)} %final_hbm.1, f32[1,1024]{1,0:T(1,128)} %cong_hbm.1, ...), custom_call_target="tpu_custom_call" | custom-call | tf_op jit(solution)/shard_map/pallas_call | solution.py:459
  18.4 0.7 %shard_map.104 = (f32[1,32,1024]{2,1,0:T(8,128)}, f32[1,1024]{1,0:T(1,128)}, f32[1,32,1024]{2,1,0:T(8,128)}) custom-call(f32[1,32,1024]{2,1,0:T(8,128)S(1)} %get-tuple-element.6.dens_in, f32[1,1024]{1,0:T(1,128)S(1)} %get-tuple-element.7.mean_in, f32[1,32,1024]{2,1,0:T(8,128)S(1)} %get-tuple-element.8.val_in), custom_call_target="tpu_custom_call" | custom-call | tf_op jit(solution)/shard_map/pallas_call | solution.py:515
